TPU v7x, 32 devices: a whole 2x2x4 slice. The times are simulated.
32 devices in a mesh: leaf: 32 (over z, y, x, core).
Axes of the slice: x: 2, y: 2, z: 4, core: 2. Of those that a mesh axis runs over, the one named last changes fastest.
Arguments:
- charges: bfloat16 [8192, 128, 128], P('leaf'), may hold values from -6 to 6
- basis_in: bfloat16 [8192, 64, 128], P('leaf'), may hold values from -0.5 to 0.5
- basis_out: bfloat16 [8192, 64, 128], P('leaf'), may hold values from -0.75 to 0.75
- transfer: bfloat16 [1024, 8, 64, 64], P('leaf'), may hold values from -0.375 to 0.375
- leaf_coupling: bfloat16 [16, 64, 64], replicated, may hold values from -0.25 to 0.25
- parent_coupling: bfloat16 [16, 64, 64], replicated, may hold values from -0.25 to 0.25
- leaf_sources: int32 [8192, 16], P('leaf'), may hold values from 0 to 511, as said below
- leaf_counts: int32 [8192], P('leaf'), may hold values from 2 to 16
- leaf_sends: int32 [32, 2, 128], replicated, may hold values from 0 to 255, as said below
- parent_sources: int32 [1024, 16], P('leaf'), may hold values from 0 to 63, as said below
- parent_counts: int32 [1024], P('leaf'), may hold values from 12 to 16
- parent_sends: int32 [32, 32], replicated, may hold values from 0 to 31
Outputs:
- potential: bfloat16 [8192, 128, 128], P('leaf')
Inputs may be any that keep to these rules, and one draw needn't show every extreme that they name: `leaf_sources`: every row of a device's leaf pool is read by some used slot of that device's leaf lists. `leaf_sends`: the 128 leaves offered in one direction are distinct. `parent_sources`: every row of a device's parent pool is read by some used slot of that device's parent lists.
All inputs are finite; a program needn't handle non-finite values.
Results may differ from a plain program's by a relative error of at most 0.007.
Values may be sent and summed in bfloat16 or wider, within the bound.
A program may use at most 256 MiB of HBM per device.

v0:
```python
import functools

import jax
import jax.numpy as jnp
from jax import lax
from jax.experimental import pallas as pl
from jax.experimental.pallas import tpu as pltpu
from jax.sharding import PartitionSpec as P

CHUNKS = 4
EARLY = 2
LOADS = 8
GROUP = 4
CODE = 1024
ANY = pl.BlockSpec(memory_space=pl.ANY)
SMEM = pl.BlockSpec(memory_space=pltpu.SMEM)
VMEM = pl.BlockSpec(memory_space=pltpu.VMEM)
CONTRACT_FIRST = (((0,), (0,)), ((), ()))
MESH = pl.DeviceIdType.MESH


def field_pair(first, second, pool, slots, stacked):
    columns = [
        jnp.concatenate([pool[slots[j, target]] for j in range(slots.shape[0])], 0) for target in (first, second)
    ]
    return jnp.dot(stacked[...], jnp.concatenate(columns, 1), preferred_element_type=jnp.float32)


def upward_kernel(
    n,
    charges_hbm,
    basis_hbm,
    transfer_hbm,
    leaf_sends,
    parent_sends,
    leaf_sources,
    leaf_counts,
    parent_sources,
    parent_counts,
    leaf_coupling,
    parent_coupling,
    far_out,
    field_out,
    list_out,
    charges,
    basis_in,
    transfer,
    up_all,
    near,
    far_stage,
    fast_stage,
    parent_all,
    parent_stage,
    parent_pool,
    down,
    field,
    stacked,
    pstacked,
    zeros,
    near_vector,
    parent_vector,
    near_slots,
    parent_slots,
    load_sem,
    far_sem,
    fast_sem,
    parent_send_sem,
    parent_recv_sem,
    zero_sem,
    field_sem,
    slot_sem,
):
    me = lax.axis_index("leaf")
    odd = lax.rem(me, 2)
    fast_target = me + 1 - 2 * odd
    far_target = me - 1 + 2 * odd
    has_far = jnp.logical_and(far_target >= 0, far_target < n)
    leaves, rank, rhs = up_all.shape
    parents = parent_all.shape[0]
    side = far_stage.shape[0]
    piece = side // CHUNKS
    part = leaves // LOADS
    bf16 = up_all.dtype

    loads = [pltpu.make_async_copy(transfer_hbm, transfer, load_sem.at[2, 0])]
    for c in range(LOADS):
        rows = pl.ds(c * part, part)
        loads.append(pltpu.make_async_copy(basis_hbm.at[rows], basis_in.at[rows], load_sem.at[0, c]))
        loads.append(pltpu.make_async_copy(charges_hbm.at[rows], charges.at[rows], load_sem.at[1, c]))
    for load in loads[1:] + loads[:1]:
        load.start()

    barrier = pltpu.get_barrier_semaphore()

    def greet(k, carry):
        pl.semaphore_signal(barrier, inc=1, device_id=(lax.rem(me + k, n),), device_id_type=MESH)
        return carry

    lax.fori_loop(1, n, greet, 0)
    early = EARLY * piece
    spare = leaves + side + early
    near[spare] = jnp.zeros((rank, rhs), bf16)
    parent_pool[parents + n] = jnp.zeros((rank, rhs), bf16)
    zeros[...] = jnp.zeros_like(zeros)
    for j in range(leaf_coupling.shape[0]):
        stacked[:, j * rank : (j + 1) * rank] = leaf_coupling[j]
    for j in range(parent_coupling.shape[0]):
        pstacked[:, j * rank : (j + 1) * rank] = parent_coupling[j]
    width = leaf_sources.shape[0]
    limit = leaf_counts[...]
    codes, used = [], []
    for j in range(width):
        source = leaf_sources[j : j + 1, :]
        valid = limit > j
        fast_row = source - (leaves + (1 - odd) * side)
        far_row = source - (leaves + odd * side)
        row = jnp.where(
            source < leaves,
            source,
            jnp.where(
                jnp.logical_and(fast_row >= 0, fast_row < side),
                leaves + fast_row,
                jnp.where(jnp.logical_and(far_row >= 0, far_row < early), leaves + side + far_row, spare),
            ),
        )
        near_vector[j : j + 1, :] = jnp.where(valid, row, spare)
        codes.append(j * CODE + far_row - early)
        used.append(jnp.logical_and(valid, jnp.logical_and(far_row >= early, far_row < side)))
    parent_vector[...] = jnp.zeros_like(parent_vector)
    parent_limit = parent_counts[...]
    for j in range(parent_sources.shape[0]):
        parent_vector[j : j + 1, 0:parents] = jnp.where(parent_limit > j, parent_sources[j : j + 1, :], parents + n)
    slot_copies = [
        pltpu.make_async_copy(near_vector, near_slots, slot_sem.at[0]),
        pltpu.make_async_copy(parent_vector, parent_slots, slot_sem.at[1]),
    ]
    for copy in slot_copies:
        copy.start()

    place = jnp.zeros_like(limit)
    places = []
    for j in range(width):
        places.append(place)
        place = place + used[j].astype(jnp.int32)
    for p in range(width):
        entry = jnp.full_like(place, side - early)
        for j in range(p, width):
            entry = jnp.where(jnp.logical_and(used[j], places[j] == p), codes[j], entry)
        list_out[p : p + 1, :] = entry
    list_out[width : width + 1, :] = place
    for copy in slot_copies:
        copy.wait()
    for load in loads[1:]:
        load.wait()
    pl.semaphore_wait(barrier, n - 1)

    def up(first, second):
        both = jnp.dot(
            jnp.concatenate([basis_in[first], basis_in[second]], 0),
            jnp.concatenate([charges[first], charges[second]], 1),
            preferred_element_type=jnp.float32,
        )
        return both[:rank, :rhs].astype(bf16), both[rank:, rhs:].astype(bf16)

    def landing(c):
        if c < EARLY:
            return near.at[pl.ds(leaves + side + c * piece, piece)]
        return far_out.at[pl.ds((c - EARLY) * piece, piece)]

    def far_copy(c):
        rows = pl.ds(c * piece, piece)
        return pltpu.make_async_remote_copy(
            src_ref=far_stage.at[rows],
            dst_ref=landing(c),
            send_sem=far_sem.at[0, c],
            recv_sem=far_sem.at[1, c],
            device_id=(far_target,),
            device_id_type=MESH,
        )

    def zero_copy(c):
        return pltpu.make_async_copy(zeros, landing(c), zero_sem.at[c])

    def send_far(c, value):
        def fill_far(i, carry):
            at = c * piece + 2 * i
            far_stage[at], far_stage[at + 1] = value(leaf_sends[me, odd, at], leaf_sends[me, odd, at + 1])
            return carry

        lax.fori_loop(0, piece // 2, fill_far, 0, unroll=4)

        @pl.when(has_far)
        def _():
            far_copy(c).start()

        @pl.when(jnp.logical_not(has_far))
        def _():
            zero_copy(c).start()

    for c in range(EARLY):
        send_far(c, up)

    def up_rows(i, carry):
        for leaf, row in zip((2 * i, 2 * i + 1), up(2 * i, 2 * i + 1)):
            up_all[leaf] = row
            near[leaf] = row
        return carry

    lax.fori_loop(0, leaves // 2, up_rows, 0, unroll=4)
    def fill_fast(i, carry):
        fast_stage[i] = up_all[leaf_sends[me, 1 - odd, i]]
        return carry

    lax.fori_loop(0, side, fill_fast, 0, unroll=4)
    fast_copy = pltpu.make_async_remote_copy(
        src_ref=fast_stage,
        dst_ref=near.at[pl.ds(leaves, side)],
        send_sem=fast_sem.at[0],
        recv_sem=fast_sem.at[1],
        device_id=(fast_target,),
        device_id_type=MESH,
    )
    fast_copy.start()

    loads[0].wait()

    def up_parent(p, carry):
        row = lax.dot_general(
            transfer[p].reshape(8 * rank, rank),
            up_all[pl.ds(8 * p, 8)].reshape(8 * rank, rhs),
            CONTRACT_FIRST,
            preferred_element_type=jnp.float32,
        ).astype(bf16)
        parent_all[p] = row
        parent_pool[p] = row
        return carry

    lax.fori_loop(0, parents, up_parent, 0, unroll=2)

    def fill_parent(d, carry):
        parent_stage[d] = parent_all[parent_sends[me, d]]
        return carry

    lax.fori_loop(0, n, fill_parent, 0)

    def parent_copy(k):
        target = lax.rem(me + k, n)
        return pltpu.make_async_remote_copy(
            src_ref=parent_stage.at[target],
            dst_ref=parent_pool.at[parents + me],
            send_sem=parent_send_sem.at[k],
            recv_sem=parent_recv_sem.at[k],
            device_id=(target,),
            device_id_type=MESH,
        )

    def start_parent(k, carry):
        parent_copy(k).start()
        return carry

    lax.fori_loop(1, n, start_parent, 0)
    parent_pool[parents + me] = parent_stage[me]

    for c in range(EARLY, CHUNKS):
        send_far(c, lambda first, second: (up_all[first], up_all[second]))
    fast_copy.wait()
    for c in range(EARLY):

        @pl.when(has_far)
        def _():
            far_copy(c).wait_recv()

        @pl.when(jnp.logical_not(has_far))
        def _():
            zero_copy(c).wait()


    def near_pair(i, carry):
        pair = field_pair(2 * i, 2 * i + 1, near, near_slots, stacked)
        field[2 * i] = pair[:, :rhs]
        field[2 * i + 1] = pair[:, rhs:]
        return carry

    lax.fori_loop(0, leaves // 2, near_pair, 0, unroll=2)

    def wait_parent(k, carry):
        source = lax.rem(me - k + n, n)
        copy = pltpu.make_async_remote_copy(
            src_ref=parent_stage.at[lax.rem(me + k, n)],
            dst_ref=parent_pool.at[parents + source],
            send_sem=parent_send_sem.at[k],
            recv_sem=parent_recv_sem.at[k],
            device_id=(lax.rem(me + k, n),),
            device_id_type=MESH,
        )
        copy.wait_send()
        copy.wait_recv()
        return carry

    lax.fori_loop(1, n, wait_parent, 0)

    def parent_pair(i, carry):
        pair = field_pair(2 * i, 2 * i + 1, parent_pool, parent_slots, pstacked)
        down[2 * i] = pair[:, :rhs].astype(bf16)
        down[2 * i + 1] = pair[:, rhs:].astype(bf16)
        return carry

    lax.fori_loop(0, parents // 2, parent_pair, 0)

    def field_copy(c):
        rows = pl.ds(c * part, part)
        return pltpu.make_async_copy(field.at[rows], field_out.at[rows], field_sem.at[c])

    for c in range(LOADS):

        def push(i, carry):
            p = c * (parents // LOADS) + i
            pushed = jnp.dot(transfer[p].reshape(8 * rank, rank), down[p], preferred_element_type=jnp.float32)
            rows = pl.ds(8 * p, 8)
            field[rows] = field[rows] + pushed.reshape(8, rank, rhs)
            return carry

        lax.fori_loop(0, parents // LOADS, push, 0, unroll=2)
        field_copy(c).start()
    for c in range(LOADS):
        field_copy(c).wait()
    for c in range(CHUNKS):

        @pl.when(has_far)
        def _():
            far_copy(c).wait_send()

    for c in range(EARLY, CHUNKS):

        @pl.when(has_far)
        def _():
            far_copy(c).wait_recv()

        @pl.when(jnp.logical_not(has_far))
        def _():
            zero_copy(c).wait()


def downward_kernel(lists, leaf_coupling, far, field, basis_out, potential, pool, even_side, odd_side, total, sem):
    step = pl.program_id(0)
    block, rank, rhs = total.shape
    side = far.shape[0]
    width = leaf_coupling.shape[0]

    @pl.when(step == 0)
    def _():
        copy = pltpu.make_async_copy(far, pool.at[pl.ds(0, side)], sem)
        copy.start()
        pool[side] = jnp.zeros((rank, rhs), pool.dtype)
        blank = jnp.zeros((rank, rank), pool.dtype)
        for j in range(width):
            even_side[j] = jnp.concatenate([leaf_coupling[j], blank], 1)
            odd_side[j] = jnp.concatenate([blank, leaf_coupling[j]], 1)
        copy.wait()

    def group(targets, g):
        left, right = [], []
        for target in targets:
            codes = [lists[GROUP * g + k, target] for k in range(GROUP)]
            slot = [lax.shift_right_logical(code, 10) for code in codes]
            sides = [even_side[slot[k]] + odd_side[slot[k + 1]] for k in range(0, GROUP, 2)]
            left.append(jnp.concatenate(sides, 1))
            right.append(jnp.concatenate([pool[jnp.bitwise_and(code, CODE - 1)] for code in codes], 0))
        product = jnp.dot(
            jnp.concatenate(left, 0), jnp.concatenate(right, 1), preferred_element_type=jnp.float32
        )
        return [product[k * rank : (k + 1) * rank, k * rhs : (k + 1) * rhs] for k in range(len(targets))]

    for leaf in range(0, block, 2):
        target = step * block + leaf
        first, second = group((target, target + 1), 0)
        total[leaf] = field[leaf] + first
        total[leaf + 1] = field[leaf + 1] + second

    def rest(leaf):
        target = step * block + leaf
        count = lists[width, target]

        @pl.when(count > GROUP)
        def _():
            def more(g, carry):
                total[leaf] += group((target,), g)[0]
                return carry

            lax.fori_loop(1, lax.shift_right_logical(count + (GROUP - 1), 2), more, 0)

    for leaf in range(block):
        rest(leaf)
    blank = jnp.zeros((rank, rhs), jnp.bfloat16)
    for leaf in range(0, block, 2):
        first, second = (total[leaf + k].astype(jnp.bfloat16) for k in range(2))
        diagonal = jnp.concatenate(
            [jnp.concatenate([first, blank], 1), jnp.concatenate([blank, second], 1)], 0
        )
        both = lax.dot_general(
            basis_out[leaf : leaf + 2].reshape(2 * rank, basis_out.shape[2]),
            diagonal,
            CONTRACT_FIRST,
            preferred_element_type=jnp.float32,
        ).astype(potential.dtype)
        potential[leaf] = both[:, :rhs]
        potential[leaf + 1] = both[:, rhs:]


def shards(
    n,
    charges,
    basis_in,
    basis_out,
    transfer,
    leaf_coupling,
    parent_coupling,
    leaf_sources,
    leaf_counts,
    leaf_sends,
    parent_sources,
    parent_counts,
    parent_sends,
):
    leaves, points, rhs = charges.shape
    rank = basis_in.shape[1]
    parents = transfer.shape[0]
    side = leaf_sends.shape[2]
    width = leaf_sources.shape[1]
    pwidth = parent_sources.shape[1]
    block = 32
    bf16 = jnp.bfloat16
    list_rows = width + 8
    early = EARLY * (side // CHUNKS)
    far, field, lists = pl.pallas_call(
        functools.partial(upward_kernel, n),
        out_shape=(
            jax.ShapeDtypeStruct((side - early, rank, rhs), bf16),
            jax.ShapeDtypeStruct((leaves, rank, rhs), jnp.float32),
            jax.ShapeDtypeStruct((list_rows, leaves), jnp.int32),
        ),
        in_specs=[ANY, ANY, ANY, SMEM, SMEM] + [VMEM] * 6,
        out_specs=(ANY, ANY, VMEM),
        scratch_shapes=[
            pltpu.VMEM((leaves, points, rhs), bf16),
            pltpu.VMEM((leaves, rank, points), bf16),
            pltpu.VMEM((parents, 8, rank, rank), bf16),
            pltpu.VMEM((leaves, rank, rhs), bf16),
            pltpu.VMEM((leaves + side + early + 1, rank, rhs), bf16),
            pltpu.VMEM((side, rank, rhs), bf16),
            pltpu.VMEM((side, rank, rhs), bf16),
            pltpu.VMEM((parents, rank, rhs), bf16),
            pltpu.VMEM((n, rank, rhs), bf16),
            pltpu.VMEM((parents + n + 1, rank, rhs), bf16),
            pltpu.VMEM((parents, rank, rhs), bf16),
            pltpu.VMEM((leaves, rank, rhs), jnp.float32),
            pltpu.VMEM((rank, width * rank), bf16),
            pltpu.VMEM((rank, pwidth * rank), bf16),
            pltpu.VMEM((side // CHUNKS, rank, rhs), bf16),
            pltpu.VMEM((width, leaves), jnp.int32),
            pltpu.VMEM((pwidth, -(-parents // 128) * 128), jnp.int32),
            pltpu.SMEM((width, leaves), jnp.int32),
            pltpu.SMEM((pwidth, -(-parents // 128) * 128), jnp.int32),
            pltpu.SemaphoreType.DMA((3, LOADS)),
            pltpu.SemaphoreType.DMA((2, CHUNKS)),
            pltpu.SemaphoreType.DMA((2,)),
            pltpu.SemaphoreType.DMA((n,)),
            pltpu.SemaphoreType.DMA((n,)),
            pltpu.SemaphoreType.DMA((CHUNKS,)),
            pltpu.SemaphoreType.DMA((LOADS,)),
            pltpu.SemaphoreType.DMA((2,)),
        ],
        compiler_params=pltpu.CompilerParams(
            collective_id=0, has_side_effects=True, vmem_limit_bytes=56 * 2**20
        ),
        name="upward",
    )(
        charges,
        basis_in,
        transfer,
        leaf_sends,
        parent_sends,
        leaf_sources.T,
        leaf_counts[None, :],
        parent_sources.T,
        parent_counts[None, :],
        leaf_coupling,
        parent_coupling,
    )
    return pl.pallas_call(
        downward_kernel,
        out_shape=jax.ShapeDtypeStruct((leaves, points, rhs), bf16),
        grid_spec=pltpu.PrefetchScalarGridSpec(
            num_scalar_prefetch=1,
            grid=(leaves // block,),
            in_specs=[
                pl.BlockSpec(leaf_coupling.shape, lambda i, *_: (0, 0, 0)),
                ANY,
                pl.BlockSpec((block, rank, rhs), lambda i, *_: (i, 0, 0)),
                pl.BlockSpec((block, rank, points), lambda i, *_: (i, 0, 0)),
            ],
            out_specs=pl.BlockSpec((block, points, rhs), lambda i, *_: (i, 0, 0)),
            scratch_shapes=[
                pltpu.VMEM((side - early + 1, rank, rhs), bf16),
                pltpu.VMEM((width, rank, 2 * rank), bf16),
                pltpu.VMEM((width, rank, 2 * rank), bf16),
                pltpu.VMEM((block, rank, rhs), jnp.float32),
                pltpu.SemaphoreType.DMA,
            ],
        ),
        compiler_params=pltpu.CompilerParams(vmem_limit_bytes=60 * 2**20),
        name="downward",
    )(lists, leaf_coupling, far, field, basis_out)


def solution(mesh):
    return jax.shard_map(
        functools.partial(shards, mesh.shape["leaf"]),
        mesh=mesh,
        in_specs=(
            P("leaf", None, None),
            P("leaf", None, None),
            P("leaf", None, None),
            P("leaf", None, None, None),
            P(),
            P(),
            P("leaf", None),
            P("leaf"),
            P(),
            P("leaf", None),
            P("leaf"),
            P(),
        ),
        out_specs=P("leaf", None, None),
        check_vma=False,
    )
```

profile of v0, /device:TPU:2, one launch (start us, length us, event | category | flops | bytes accessed | tf_op | source)
XLA Modules:
  0.0 95.3 jit_solution(18355061947273783811)
XLA Ops:
  0.0 77.1 %upward.1 = (bf16[64,64,128]{2,1,0:T(8,128)(2,1)}, f32[256,64,128]{2,1,0:T(8,128)}, s32[24,256]{1,0:T(8,128)}) custom-call(bf16[256,128,128]{2,1,0:T(8,128)(2,1)} %charges_hbm.1, bf16[256,64,128]{2,1,0:T(8,128)(2,1)} %basis_hbm.1, bf16[32,8,64,64]{3,2,1,0:T(8,128)(2,1)} %transfer_hbm.1, s32[32,2,128]{2,1,0:T(2,128)} %leaf_sends.1, s32[32,32]{1,0:T(8,128)} %parent_sends.1, ...), custom_call_target="tpu_custom_call" | custom-call | tf_op jit(solution)/shard_map/upward/pallas_call | solution.py:435
  77.1 18.2 %downward.1 = bf16[256,128,128]{2,1,0:T(8,128)(2,1)} custom-call(s32[24,256]{1,0:T(8,128)} %get-tuple-element.8.lists, bf16[16,64,64]{2,1,0:T(8,128)(2,1)} %leaf_coupling.3, bf16[64,64,128]{2,1,0:T(8,128)(2,1)} %get-tuple-element.9.far, f32[256,64,128]{2,1,0:T(8,128)} %get-tuple-element.10.field, bf16[256,64,128]{2,1,0:T(8,128)(2,1)} %basis_out.1), custom_call_target="tpu_custom_call" | custom-call | tf_op jit(solution)/shard_map/downward/pallas_call | solution.py:490
where the time goes:
time: 96 us; the launch traced here: 95.3 us
  Pallas kernels  95.3 us (99%)
    pallas_call x1, Pallas kernels, shards(): pl.pallas_call(functools.partial(upward_kernel, n), out_shape=(jax.ShapeD...  77.1 us
    pallas_call x1, Pallas kernels, shards(): pl.pallas_call(downward_kernel, out_shape=jax.ShapeDtypeStruct((leaves, p...  18.2 us

commit v1 on v0

--- a/solution.py
+++ b/solution.py
@@ -8,7 +8,7 @@
 from jax.sharding import PartitionSpec as P
 
 CHUNKS = 4
-EARLY = 2
+EARLY = 1
 LOADS = 8
 GROUP = 4
 CODE = 1024

time: 96 us -> 83 us (0.86)
  the two profiles are of different devices: /device:TPU:2 before, /device:TPU:1 now
where the time goes in v1:
time: 83 us; the launch traced here: 82.7 us
  Pallas kernels  82.7 us (100%)
    pallas_call x1, Pallas kernels, shards(): pl.pallas_call(functools.partial(upward_kernel, n), out_shape=(jax.ShapeD...  63.1 us
    pallas_call x1, Pallas kernels, shards(): pl.pallas_call(downward_kernel, out_shape=jax.ShapeDtypeStruct((leaves, p...  19.6 us

profile of v1, /device:TPU:1, one launch (start us, length us, event | category | flops | bytes accessed | tf_op | source)
XLA Modules:
  0.0 82.7 jit_solution(10439579506072924440)
XLA Ops:
  0.0 63.1 %upward.1 = (bf16[96,64,128]{2,1,0:T(8,128)(2,1)}, f32[256,64,128]{2,1,0:T(8,128)}, s32[24,256]{1,0:T(8,128)}) custom-call(bf16[256,128,128]{2,1,0:T(8,128)(2,1)} %charges_hbm.1, bf16[256,64,128]{2,1,0:T(8,128)(2,1)} %basis_hbm.1, bf16[32,8,64,64]{3,2,1,0:T(8,128)(2,1)} %transfer_hbm.1, s32[32,2,128]{2,1,0:T(2,128)} %leaf_sends.1, s32[32,32]{1,0:T(8,128)} %parent_sends.1, ...), custom_call_target="tpu_custom_call" | custom-call | tf_op jit(solution)/shard_map/upward/pallas_call | solution.py:435
  63.1 19.6 %downward.1 = bf16[256,128,128]{2,1,0:T(8,128)(2,1)} custom-call(s32[24,256]{1,0:T(8,128)} %get-tuple-element.8.lists, bf16[16,64,64]{2,1,0:T(8,128)(2,1)} %leaf_coupling.3, bf16[96,64,128]{2,1,0:T(8,128)(2,1)} %get-tuple-element.9.far, f32[256,64,128]{2,1,0:T(8,128)} %get-tuple-element.10.field, bf16[256,64,128]{2,1,0:T(8,128)(2,1)} %basis_out.1), custom_call_target="tpu_custom_call" | custom-call | tf_op jit(solution)/shard_map/downward/pallas_call | solution.py:490
